TPU v7x, 256 devices: a whole 4x4x8 slice. The times are simulated.
256 devices in a mesh: ctx: 16 (over x, y_hi, core), head: 16 (over y_lo, z).
Axes of the slice: x: 4, y: 4 (y_hi: 2, y_lo: 2; y = y_hi * 2 + y_lo), z: 8, core: 2. Of those that a mesh axis runs over, the one named last changes fastest.
Arguments:
- queries: bfloat16 [8192, 7168], P(('ctx', 'head')), may hold values from -120 to 120, as said below
- keys: bfloat16 [8192, 1024], P(('ctx', 'head')), may hold values from -5 to 5, as said below
- values: bfloat16 [8192, 1024], P(('ctx', 'head')), may hold values from -6 to 6
- order: int32 [32], replicated, may hold values from 0 to 31, each once
Outputs:
- attended: bfloat16 [8192, 7168], P(('ctx', 'head'))
Inputs may be any that keep to these rules, and one draw needn't show every extreme that they name: `queries`: each query row lies within the bound. `keys`: each key entry lies within the bound.
All inputs are finite; a program needn't handle non-finite values.
Results may differ from a plain program's by a relative error of at most 0.006.
Values may be sent and summed in bfloat16 or wider, within the bound.
A program may use at most 128 MiB of HBM per device.

v0:
```python
import jax
import jax.numpy as jnp
from jax import lax
from jax.sharding import PartitionSpec as P

HD = 128
QH = 56
KVH = 8
BLK = 256


def seq_positions(rows, order):
    ids = rows // BLK
    table = jnp.sum(
        jnp.where(
            ids[:, None] == jnp.arange(order.shape[0], dtype=jnp.int32)[None, :], order[None, :], 0
        ),
        axis=1,
    )
    return table * BLK + rows % BLK


def step_width(length):
    for candidate in (1024, 768, 512, 384, 256, 128):
        return candidate
    return length


def shards(queries, keys, values, order):
    n_head = lax.axis_size("head")
    ctx_index = lax.axis_index("ctx")
    rows_in = queries.shape[0]
    block_rows = rows_in * n_head
    group = QH // KVH
    copies = n_head // KVH
    held = 1
    subset = (group + copies - 1) // copies
    padded_group = subset * copies
    split_queries = queries.reshape(rows_in, KVH, group, HD)
    split_queries = jnp.pad(split_queries, ((0, 0), (0, 0), (0, padded_group - group), (0, 0)))
    outgoing = split_queries.reshape(rows_in, KVH // held, held, copies, subset, HD)
    outgoing = jnp.transpose(outgoing, (1, 3, 0, 2, 4, 5)).reshape(
        n_head, 1, rows_in, held * subset * HD
    )
    arrived = lax.all_to_all(outgoing, "head", split_axis=0, concat_axis=1, tiled=True)
    local_queries = arrived.reshape(block_rows, held, subset, HD)
    kv_dev = held * subset
    key_heads = jnp.broadcast_to(keys.reshape(rows_in, KVH, 1, HD), (rows_in, KVH, subset, HD))
    value_heads = jnp.broadcast_to(values.reshape(rows_in, KVH, 1, HD), (rows_in, KVH, subset, HD))

    def arrange(heads):
        width_heads = heads.shape[2]
        shaped = heads.reshape(rows_in, KVH // held, 1, held * width_heads, HD)
        shaped = jnp.broadcast_to(shaped, (rows_in, KVH // held, copies, held * width_heads, HD))
        return jnp.transpose(shaped, (1, 2, 0, 3, 4)).reshape(
            n_head, 1, rows_in, held * width_heads * HD
        )

    local_keys, local_values = (
        lax.all_to_all(arrange(key_heads), "head", split_axis=0, concat_axis=1, tiled=True),
        lax.all_to_all(arrange(value_heads), "head", split_axis=0, concat_axis=1, tiled=True),
    )
    local_keys = local_keys.reshape(block_rows, kv_dev, HD)
    local_values = local_values.reshape(block_rows, kv_dev, HD)
    local_rows = jnp.arange(block_rows, dtype=jnp.int32)
    query_pos = seq_positions(ctx_index * block_rows + local_rows, order)
    last_query = jnp.max(query_pos)
    scale = HD ** (-0.5)
    initial = (
        jnp.full((held, subset, block_rows), -1e30, jnp.float32),
        jnp.zeros((held, subset, block_rows), jnp.float32),
        jnp.zeros((held, subset, block_rows, HD), jnp.float32),
    )
    key_piece = lax.all_gather(local_keys, "ctx", axis=0, tiled=True)
    value_piece = lax.all_gather(local_values, "ctx", axis=0, tiled=True)
    length = key_piece.shape[0]
    width = step_width(length)
    steps = length // width
    key_steps = key_piece.reshape(steps, width, kv_dev, HD)
    value_steps = value_piece.reshape(steps, width, kv_dev, HD)

    def one_step(state, inputs):
        key_block, value_block, step_index = inputs
        key_pos = seq_positions(step_index * width + jnp.arange(width, dtype=jnp.int32), order)

        def update(current):
            top, total, accum = current
            key_four = key_block.reshape(width, held, subset, HD)
            value_four = value_block.reshape(width, held, subset, HD)
            score = (
                jnp.einsum(
                    "qgjd,kgjd->gjqk", local_queries, key_four, preferred_element_type=jnp.float32
                )
                * scale
            )
            kept = key_pos[None, :] <= query_pos[:, None]
            block_top = jnp.max(jnp.where(kept, score, -1e30), axis=-1)
            new_top = jnp.maximum(top, block_top)
            weight = jnp.where(kept, jnp.exp(score - new_top[..., None]), 0.0)
            factor = jnp.exp(top - new_top)
            new_total = total * factor + jnp.sum(weight, axis=-1)
            mixed = jnp.einsum(
                "gjqk,kgjd->gjqd",
                weight.astype(jnp.bfloat16),
                value_four,
                preferred_element_type=jnp.float32,
            )
            return (new_top, new_total, accum * factor[..., None] + mixed)

        state = lax.cond(jnp.min(key_pos) <= last_query, update, lambda current: current, state)
        return (state, None)

    result, unused = lax.scan(
        one_step, initial, (key_steps, value_steps, jnp.arange(steps, dtype=jnp.int32))
    )
    top, total, accum = result
    output = (accum / total[..., None]).astype(jnp.bfloat16)
    output = jnp.transpose(output, (2, 0, 1, 3)).reshape(1, n_head, rows_in, held * subset * HD)
    returned = lax.all_to_all(output, "head", split_axis=1, concat_axis=0, tiled=True)
    returned = returned.reshape(KVH // held, copies, rows_in, held, subset, HD)
    returned = jnp.transpose(returned, (2, 0, 3, 1, 4, 5)).reshape(rows_in, KVH, padded_group, HD)
    joined = returned[:, :, :group, :]
    return joined.reshape(rows_in, QH * HD)


def solution(mesh):
    in_specs = (P(("ctx", "head"), None), P(("ctx", "head"), None), P(("ctx", "head"), None), P())
    out_specs = P(("ctx", "head"), None)
    return jax.shard_map(shards, mesh=mesh, in_specs=in_specs, out_specs=out_specs, check_vma=False)
```

profile of v0, /device:TPU:25, one launch (start us, length us, event | category | flops | bytes accessed | tf_op | source)
XLA Modules:
  0.0 328.5 jit_solution(17382368687177497994)
XLA Ops:
  6.5 0.8 copy-done
  7.8 21.3 %all_to_all.16 = bf16[16,1,32,512]{3,2,1,0:T(8,128)(2,1)S(1)} all-to-all(bf16[16,1,32,512]{3,2,1,0:T(8,128)(2,1)S(1)} %reshape.150), channel_id=1, replica_groups=mesh['ctx'=16,'head'=16] {'head'}, dimensions={0} | all-to-all | bytes 1048576 | tf_op jit(solution)/shard_map/all_to_all | solution.py:60
  29.2 0.9 reshape.151
  30.1 0.9 copy_bitcast_fusion
  31.4 19.5 %all_to_all.17 = bf16[16,1,32,512]{3,2,1,0:T(8,128)(2,1)S(1)} all-to-all(bf16[16,1,32,512]{3,2,1,0:T(8,128)(2,1)S(1)} %reshape.157), channel_id=1, replica_groups=mesh['ctx'=16,'head'=16] {'head'}, dimensions={0} | all-to-all | bytes 1048576 | tf_op jit(solution)/shard_map/all_to_all | solution.py:61
  50.9 1.0 reshape.158
  52.9 1.1 copy.44
  54.0 7.0 %all-to-all-start.1 = ((bf16[16,1,32,512]{3,2,1,0:T(8,128)(2,1)}), bf16[16,1,32,512]{3,2,1,0:T(8,128)(2,1)S(1)}, u32[]{:S(2)}, u32[]{:S(2)}) async-start(bf16[16,1,32,512]{3,2,1,0:T(8,128)(2,1)} %copy.44), calls=%async_computation.1 | async-start | bytes 1048576 | tf_op jit(solution)/shard_map/all_to_all | solution.py:45
  61.7 11.1 %all-to-all-done.1 = bf16[16,1,32,512]{3,2,1,0:T(8,128)(2,1)S(1)} async-done(((bf16[16,1,32,512]{3,2,1,0:T(8,128)(2,1)}), bf16[16,1,32,512]{3,2,1,0:T(8,128)(2,1)S(1)}, u32[]{:S(2)}, u32[]{:S(2)}) %all-to-all-start.1) | async-done | bytes 524320 | tf_op jit(solution)/shard_map/all_to_all | solution.py:45
  73.0 38.1 %all-gather.3.cloned.1.call-done = bf16[8192,4,128]{2,1,0:T(4,128)(2,1)} async-done(((bf16[512,4,128]{2,1,0:T(4,128)(2,1)}), bf16[8192,4,128]{2,1,0:T(4,128)(2,1)}) %all-gather.3.cloned.1.call-update) | async-done | bytes 8388624 | tf_op jit(solution)/shard_map/all_gather | solution.py:74
  111.1 8.7 %copy.35 = bf16[8,1024,4,128]{3,1,2,0:T(8,128)(2,1)} copy(bf16[8,1024,4,128]{3,2,1,0:T(4,128)(2,1)} %bitcast.86) | data formatting | bytes 16777216 | tf_op jit(solution)/shard_map/while | solution.py:113
  119.8 69.0 %all-gather.5.cloned.1.call-done = bf16[8192,4,128]{2,1,0:T(4,128)(2,1)} async-done(((bf16[512,4,128]{2,1,0:T(4,128)(2,1)}), bf16[8192,4,128]{2,1,0:T(4,128)(2,1)}) %all-gather.5.cloned.1.call-update) | async-done | bytes 8388624 | tf_op jit(solution)/shard_map/all_gather | solution.py:75
  188.8 8.7 %copy.37 = bf16[8,1024,4,128]{3,1,2,0:T(8,128)(2,1)} copy(bf16[8,1024,4,128]{3,2,1,0:T(4,128)(2,1)} %bitcast.87) | data formatting | bytes 16777216 | tf_op jit(solution)/shard_map/while | solution.py:113
  197.6 101.1 %while.16 = (s32[]{:T(128)}, f32[1,4,512]{2,1,0:T(4,128)S(1)}, f32[1,4,512]{2,1,0:T(4,128)S(1)}, f32[1,4,512,128]{3,2,1,0:T(8,128)S(1)}, s32[8]{0:T(128)S(1)}, /...) while((s32[]{:T(128)}, f32[1,4,512]{2,1,0:T(4,128)S(1)}, ...), condition=%wide.region_9.10_spmd, body=%wide.region_2.9_spmd.sunk | while | flops 1097994240 | bytes 32140720 | solution.py:113
  200.8 9.4 %conditional.2 = ((f32[1,4,512]{2,1,0:T(4,128)S(1)}, f32[1,4,512]{2,1,0:T(4,128)S(1)}, f32[1,4,512,128]{3,2,1,0:T(8,128)S(1)})) conditional(s32[]{:T(128)} %convert_element_type.28, (f32[1,4,512]{2,1,0:T(4,128)S(1)}, f32[1,4,512]{2,1,0:T(4,128)S(1)}, f32[1,4,512,128]{3,2,1,0:T(8,128)S(1)}) %tuple.50, (s32[1024]{0:T(1024)S(1)}, s32[512]{0:T(512)S(1)}, ...), branch_computations={%region_5.5_spmd, %region_6.8_spmd} | conditional | flops 1097865216 | bytes 32119840 | solution.py:110
  201.2 2.8 fusion
  204.0 4.3 %fusion.11 = f32[1,4,512,128]{3,2,1,0:T(8,128)S(1)} fusion(f32[4,1024,512]{2,1,0:T(8,128)S(1)} %get-tuple-element.299, f32[4,512]{1,0:T(4,128)S(1)} %bitcast.88, pred[512,1024]{0,1:T(8,128)(4,1)S(1)} %broadcast_compare_fusion, bf16[8,1024,4,128]{3,1,2,0:T(8,128)(2,1)} %get-tuple-element.217, s32[]{:T(128)} %get-tuple-element.213, ...), kind=kOutput, calls=%fused_computation.10 | convolution fusion | flops 545783808 | bytes 12075520 | tf_op jit(solution)/shard_map/while/body/eval_jaxpr/cond/branch_1_fun/gjqk,kgjd->gjqd/dot_general | solution.py:102
  208.3 1.8 fusion.4
  213.4 9.4 %conditional.2 = ((f32[1,4,512]{2,1,0:T(4,128)S(1)}, f32[1,4,512]{2,1,0:T(4,128)S(1)}, f32[1,4,512,128]{3,2,1,0:T(8,128)S(1)})) conditional(s32[]{:T(128)} %convert_element_type.28, (f32[1,4,512]{2,1,0:T(4,128)S(1)}, f32[1,4,512]{2,1,0:T(4,128)S(1)}, f32[1,4,512,128]{3,2,1,0:T(8,128)S(1)}) %tuple.50, (s32[1024]{0:T(1024)S(1)}, s32[512]{0:T(512)S(1)}, ...), branch_computations={%region_5.5_spmd, %region_6.8_spmd} | conditional | flops 1097865216 | bytes 32119840 | solution.py:110
  213.8 2.8 fusion
  216.6 4.3 %fusion.11 = f32[1,4,512,128]{3,2,1,0:T(8,128)S(1)} fusion(f32[4,1024,512]{2,1,0:T(8,128)S(1)} %get-tuple-element.299, f32[4,512]{1,0:T(4,128)S(1)} %bitcast.88, pred[512,1024]{0,1:T(8,128)(4,1)S(1)} %broadcast_compare_fusion, bf16[8,1024,4,128]{3,1,2,0:T(8,128)(2,1)} %get-tuple-element.217, s32[]{:T(128)} %get-tuple-element.213, ...), kind=kOutput, calls=%fused_computation.10 | convolution fusion | flops 545783808 | bytes 12075520 | tf_op jit(solution)/shard_map/while/body/eval_jaxpr/cond/branch_1_fun/gjqk,kgjd->gjqd/dot_general | solution.py:102
  221.0 1.8 fusion.4
  226.1 9.4 %conditional.2 = ((f32[1,4,512]{2,1,0:T(4,128)S(1)}, f32[1,4,512]{2,1,0:T(4,128)S(1)}, f32[1,4,512,128]{3,2,1,0:T(8,128)S(1)})) conditional(s32[]{:T(128)} %convert_element_type.28, (f32[1,4,512]{2,1,0:T(4,128)S(1)}, f32[1,4,512]{2,1,0:T(4,128)S(1)}, f32[1,4,512,128]{3,2,1,0:T(8,128)S(1)}) %tuple.50, (s32[1024]{0:T(1024)S(1)}, s32[512]{0:T(512)S(1)}, ...), branch_computations={%region_5.5_spmd, %region_6.8_spmd} | conditional | flops 1097865216 | bytes 32119840 | solution.py:110
  226.4 2.8 fusion
  229.3 4.3 %fusion.11 = f32[1,4,512,128]{3,2,1,0:T(8,128)S(1)} fusion(f32[4,1024,512]{2,1,0:T(8,128)S(1)} %get-tuple-element.299, f32[4,512]{1,0:T(4,128)S(1)} %bitcast.88, pred[512,1024]{0,1:T(8,128)(4,1)S(1)} %broadcast_compare_fusion, bf16[8,1024,4,128]{3,1,2,0:T(8,128)(2,1)} %get-tuple-element.217, s32[]{:T(128)} %get-tuple-element.213, ...), kind=kOutput, calls=%fused_computation.10 | convolution fusion | flops 545783808 | bytes 12075520 | tf_op jit(solution)/shard_map/while/body/eval_jaxpr/cond/branch_1_fun/gjqk,kgjd->gjqd/dot_general | solution.py:102
  233.6 1.8 fusion.4
  238.7 9.4 %conditional.2 = ((f32[1,4,512]{2,1,0:T(4,128)S(1)}, f32[1,4,512]{2,1,0:T(4,128)S(1)}, f32[1,4,512,128]{3,2,1,0:T(8,128)S(1)})) conditional(s32[]{:T(128)} %convert_element_type.28, (f32[1,4,512]{2,1,0:T(4,128)S(1)}, f32[1,4,512]{2,1,0:T(4,128)S(1)}, f32[1,4,512,128]{3,2,1,0:T(8,128)S(1)}) %tuple.50, (s32[1024]{0:T(1024)S(1)}, s32[512]{0:T(512)S(1)}, ...), branch_computations={%region_5.5_spmd, %region_6.8_spmd} | conditional | flops 1097865216 | bytes 32119840 | solution.py:110
  239.1 2.8 fusion
  241.9 4.3 %fusion.11 = f32[1,4,512,128]{3,2,1,0:T(8,128)S(1)} fusion(f32[4,1024,512]{2,1,0:T(8,128)S(1)} %get-tuple-element.299, f32[4,512]{1,0:T(4,128)S(1)} %bitcast.88, pred[512,1024]{0,1:T(8,128)(4,1)S(1)} %broadcast_compare_fusion, bf16[8,1024,4,128]{3,1,2,0:T(8,128)(2,1)} %get-tuple-element.217, s32[]{:T(128)} %get-tuple-element.213, ...), kind=kOutput, calls=%fused_computation.10 | convolution fusion | flops 545783808 | bytes 12075520 | tf_op jit(solution)/shard_map/while/body/eval_jaxpr/cond/branch_1_fun/gjqk,kgjd->gjqd/dot_general | solution.py:102
  246.2 1.8 fusion.4
  251.3 9.4 %conditional.2 = ((f32[1,4,512]{2,1,0:T(4,128)S(1)}, f32[1,4,512]{2,1,0:T(4,128)S(1)}, f32[1,4,512,128]{3,2,1,0:T(8,128)S(1)})) conditional(s32[]{:T(128)} %convert_element_type.28, (f32[1,4,512]{2,1,0:T(4,128)S(1)}, f32[1,4,512]{2,1,0:T(4,128)S(1)}, f32[1,4,512,128]{3,2,1,0:T(8,128)S(1)}) %tuple.50, (s32[1024]{0:T(1024)S(1)}, s32[512]{0:T(512)S(1)}, ...), branch_computations={%region_5.5_spmd, %region_6.8_spmd} | conditional | flops 1097865216 | bytes 32119840 | solution.py:110
  251.7 2.8 fusion
  254.5 4.3 %fusion.11 = f32[1,4,512,128]{3,2,1,0:T(8,128)S(1)} fusion(f32[4,1024,512]{2,1,0:T(8,128)S(1)} %get-tuple-element.299, f32[4,512]{1,0:T(4,128)S(1)} %bitcast.88, pred[512,1024]{0,1:T(8,128)(4,1)S(1)} %broadcast_compare_fusion, bf16[8,1024,4,128]{3,1,2,0:T(8,128)(2,1)} %get-tuple-element.217, s32[]{:T(128)} %get-tuple-element.213, ...), kind=kOutput, calls=%fused_computation.10 | convolution fusion | flops 545783808 | bytes 12075520 | tf_op jit(solution)/shard_map/while/body/eval_jaxpr/cond/branch_1_fun/gjqk,kgjd->gjqd/dot_general | solution.py:102
  258.9 1.8 fusion.4
  264.0 9.4 %conditional.2 = ((f32[1,4,512]{2,1,0:T(4,128)S(1)}, f32[1,4,512]{2,1,0:T(4,128)S(1)}, f32[1,4,512,128]{3,2,1,0:T(8,128)S(1)})) conditional(s32[]{:T(128)} %convert_element_type.28, (f32[1,4,512]{2,1,0:T(4,128)S(1)}, f32[1,4,512]{2,1,0:T(4,128)S(1)}, f32[1,4,512,128]{3,2,1,0:T(8,128)S(1)}) %tuple.50, (s32[1024]{0:T(1024)S(1)}, s32[512]{0:T(512)S(1)}, ...), branch_computations={%region_5.5_spmd, %region_6.8_spmd} | conditional | flops 1097865216 | bytes 32119840 | solution.py:110
  264.3 2.8 fusion
  267.2 4.3 %fusion.11 = f32[1,4,512,128]{3,2,1,0:T(8,128)S(1)} fusion(f32[4,1024,512]{2,1,0:T(8,128)S(1)} %get-tuple-element.299, f32[4,512]{1,0:T(4,128)S(1)} %bitcast.88, pred[512,1024]{0,1:T(8,128)(4,1)S(1)} %broadcast_compare_fusion, bf16[8,1024,4,128]{3,1,2,0:T(8,128)(2,1)} %get-tuple-element.217, s32[]{:T(128)} %get-tuple-element.213, ...), kind=kOutput, calls=%fused_computation.10 | convolution fusion | flops 545783808 | bytes 12075520 | tf_op jit(solution)/shard_map/while/body/eval_jaxpr/cond/branch_1_fun/gjqk,kgjd->gjqd/dot_general | solution.py:102
  271.5 1.8 fusion.4
  276.6 9.4 %conditional.2 = ((f32[1,4,512]{2,1,0:T(4,128)S(1)}, f32[1,4,512]{2,1,0:T(4,128)S(1)}, f32[1,4,512,128]{3,2,1,0:T(8,128)S(1)})) conditional(s32[]{:T(128)} %convert_element_type.28, (f32[1,4,512]{2,1,0:T(4,128)S(1)}, f32[1,4,512]{2,1,0:T(4,128)S(1)}, f32[1,4,512,128]{3,2,1,0:T(8,128)S(1)}) %tuple.50, (s32[1024]{0:T(1024)S(1)}, s32[512]{0:T(512)S(1)}, ...), branch_computations={%region_5.5_spmd, %region_6.8_spmd} | conditional | flops 1097865216 | bytes 32119840 | solution.py:110
  277.0 2.8 fusion
  279.8 4.3 %fusion.11 = f32[1,4,512,128]{3,2,1,0:T(8,128)S(1)} fusion(f32[4,1024,512]{2,1,0:T(8,128)S(1)} %get-tuple-element.299, f32[4,512]{1,0:T(4,128)S(1)} %bitcast.88, pred[512,1024]{0,1:T(8,128)(4,1)S(1)} %broadcast_compare_fusion, bf16[8,1024,4,128]{3,1,2,0:T(8,128)(2,1)} %get-tuple-element.217, s32[]{:T(128)} %get-tuple-element.213, ...), kind=kOutput, calls=%fused_computation.10 | convolution fusion | flops 545783808 | bytes 12075520 | tf_op jit(solution)/shard_map/while/body/eval_jaxpr/cond/branch_1_fun/gjqk,kgjd->gjqd/dot_general | solution.py:102
  284.1 1.8 fusion.4
  289.2 9.4 %conditional.2 = ((f32[1,4,512]{2,1,0:T(4,128)S(1)}, f32[1,4,512]{2,1,0:T(4,128)S(1)}, f32[1,4,512,128]{3,2,1,0:T(8,128)S(1)})) conditional(s32[]{:T(128)} %convert_element_type.28, (f32[1,4,512]{2,1,0:T(4,128)S(1)}, f32[1,4,512]{2,1,0:T(4,128)S(1)}, f32[1,4,512,128]{3,2,1,0:T(8,128)S(1)}) %tuple.50, (s32[1024]{0:T(1024)S(1)}, s32[512]{0:T(512)S(1)}, ...), branch_computations={%region_5.5_spmd, %region_6.8_spmd} | conditional | flops 1097865216 | bytes 32119840 | solution.py:110
  289.6 2.8 fusion
  292.4 4.3 %fusion.11 = f32[1,4,512,128]{3,2,1,0:T(8,128)S(1)} fusion(f32[4,1024,512]{2,1,0:T(8,128)S(1)} %get-tuple-element.299, f32[4,512]{1,0:T(4,128)S(1)} %bitcast.88, pred[512,1024]{0,1:T(8,128)(4,1)S(1)} %broadcast_compare_fusion, bf16[8,1024,4,128]{3,1,2,0:T(8,128)(2,1)} %get-tuple-element.217, s32[]{:T(128)} %get-tuple-element.213, ...), kind=kOutput, calls=%fused_computation.10 | convolution fusion | flops 545783808 | bytes 12075520 | tf_op jit(solution)/shard_map/while/body/eval_jaxpr/cond/branch_1_fun/gjqk,kgjd->gjqd/dot_general | solution.py:102
  296.8 1.8 fusion.4
  299.6 20.4 %all_to_all.18 = bf16[1,16,32,512]{3,2,0,1:T(8,128)(2,1)S(1)} all-to-all(bf16[1,16,32,512]{3,2,0,1:T(8,128)(2,1)S(1)} %bitcast.91), channel_id=1, replica_groups=mesh['ctx'=16,'head'=16] {'head'}, dimensions={1} | all-to-all | bytes 1048576 | tf_op jit(solution)/shard_map/all_to_all | solution.py:119
  320.4 1.3 reshape.163
  (95 shorter events, 18.5 us)
Async XLA Ops:
  6.5 0.8 copy-start
  6.5 45.4 %copy-start.1 = (bf16[32,7168]{1,0:T(8,128)(2,1)S(1)}, bf16[32,7168]{1,0:T(8,128)(2,1)}, u32[]{:S(2)}) copy-start(bf16[32,7168]{1,0:T(8,128)(2,1)} %param.8) | copy-start | bytes 1376260
  6.5 54.5 %copy-start.2 = (s32[32]{0:T(128)S(1)}, s32[32]{0:T(128)}, u32[]{:S(2)}) copy-start(s32[32]{0:T(128)} %param.11) | copy-start | bytes 388
  6.5 104.6 %all-gather.3.cloned.1.call-start = ((), (), s32[]{:S(2)}) async-start(), calls=%async_computation.4 | async-start | bytes 8912896 | tf_op jit(solution)/shard_map/all_gather | solution.py:74
  30.1 158.7 %all-gather.5.cloned.1.call-start = ((), (), s32[]{:S(2)}) async-start(), calls=%async_computation.5 | async-start | bytes 8912896 | tf_op jit(solution)/shard_map/all_gather | solution.py:75
  54.0 18.9 %all-to-all-start.1 = ((bf16[16,1,32,512]{3,2,1,0:T(8,128)(2,1)}), bf16[16,1,32,512]{3,2,1,0:T(8,128)(2,1)S(1)}, u32[]{:S(2)}, u32[]{:S(2)}) async-start(bf16[16,1,32,512]{3,2,1,0:T(8,128)(2,1)} %copy.44), calls=%async_computation.1 | async-start | bytes 1048576 | tf_op jit(solution)/shard_map/all_to_all | solution.py:45
Sparse Core Ops, SparseCore 0:
  30.2 80.8 all-gather.2
  113.8 74.9 all-gather.4
where the time goes:
time: 334 us; the launch traced here: 329 us
  waiting for transfers between devices  118 us (35%)
  blocking collectives  61.2 us (18%)
  matrix products  57 us (17%)
  local copies, waits for them, and re-layouts  31.3 us (9%)
  other arithmetic  25.1 us (8%)
  loops' own time  15.1 us (5%)
  between operations  13.6 us (4%)
  starting transfers between devices  7.08 us (2%)
    all_gather x1, waiting for transfers between devices, shards(): value_piece = lax.all_gather(local_values, 'ctx', axis=0, tiled=True)  69 us
    all_gather x1, waiting for transfers between devices, shards(): key_piece = lax.all_gather(local_keys, 'ctx', axis=0, tiled=True)  38.1 us
    dot_general x8, matrix products, update(): jnp.einsum('gjqk,kgjd->gjqd', weight.astype(jnp.bfloat16), value_four, pr...  34.6 us
    dot_general x8, matrix products, update(): jnp.einsum('qgjd,kgjd->gjqk', local_queries, key_four, preferred_element_...  22.4 us
    all_to_all x1, blocking collectives, shards(): lax.all_to_all(arrange(key_heads), 'head', split_axis=0, concat_axis=1, t...  21.3 us
    all_to_all x1, blocking collectives, shards(): lax.all_to_all(output, 'head', split_axis=1, concat_axis=0, tiled=True)  20.4 us
    all_to_all x1, blocking collectives, shards(): lax.all_to_all(arrange(value_heads), 'head', split_axis=0, concat_axis=1,...  19.5 us
    while x3, local copies, waits for them, and re-layouts, shards(): lax.scan(one_step, initial, (key_steps, value_steps, jnp.arange(steps, dt...  17.4 us
  transfers between devices with their start and end apart: 3, of which 3 were waited for; matrix products, arithmetic and copies ran while one was open for 4% of the time, Pallas kernels for 0%

commit v1 on v0

v1 whole, which is shorter than its diff:
```python
import jax
import jax.numpy as jnp
from jax import lax
from jax.experimental import pallas as pl
from jax.experimental.pallas import tpu as pltpu
from jax.sharding import PartitionSpec as P

MESH = pl.DeviceIdType.MESH
HD = 128
GROUP = 7
PLANES = 8
BLOCKS = 32
PART = 32
ROWS = 8
BLK = 256
QROWS = GROUP * ROWS
QALL = BLOCKS * QROWS
CHUNK = BLOCKS * PART
WIDE = GROUP * HD
TILE = 256
TILES = QALL // TILE
VROWS = HD + 16
SCALE = HD**-0.5 * 1.4426950408889634
LOW = -1e30

SPAN = [
    ((TILE * t) // QROWS * PART, ((TILE * t + TILE - 1) // QROWS + 1) * PART) for t in range(TILES)
]
EDGE = max(last - first for first, last in SPAN)


def kernel(
    order, block_at, q_in, k_in, v_in, out,
    q_buf, raw, kv, qs, ones, acc, top, bias, result, o_buf,
    q_send, q_recv, q_own, kv_send, kv_recv, kv_own,
    up_send, up_recv, down_send, down_recv, near_send, near_recv,
    o_send, o_recv, o_own,
):
    ctx = lax.axis_index("ctx")
    head = lax.axis_index("head")
    z = lax.rem(head, PLANES)
    y_lo = head // PLANES
    core = lax.rem(ctx, 2)
    g = ctx // 2
    part = 2 * y_lo + core
    me = 2 * ctx + y_lo
    sibling = (ctx + 1 - 2 * core, head)
    above = (ctx, y_lo * PLANES + lax.rem(z + 1, PLANES))
    below = (ctx, y_lo * PLANES + lax.rem(z + PLANES - 1, PLANES))

    def plane_device(index):
        return (index // 2, lax.rem(index, 2) * PLANES + z)

    barrier = pltpu.get_barrier_semaphore()

    def greet(i, carry):
        pl.semaphore_signal(
            barrier, inc=1, device_id=plane_device(lax.rem(me + i, 32)), device_id_type=MESH
        )
        return carry

    lax.fori_loop(1, 32, greet, 0)
    for device in (above, below):
        pl.semaphore_signal(barrier, inc=1, device_id=device, device_id_type=MESH)

    own_q = pltpu.make_async_copy(
        q_in.at[part, :, pl.ds(pl.multiple_of(g * WIDE, HD), WIDE)], q_buf.at[me], q_own
    )
    own_q.start()

    def for_core(of, do):
        for which, source in ((0, k_in), (1, v_in)):
            pl.when(of == which)(lambda source=source: do(source))

    own_columns = pl.ds(pl.multiple_of(g * HD, HD), HD)
    for_core(
        core, lambda source: pltpu.make_async_copy(source.at[:, own_columns], raw.at[me], kv_own).start()
    )

    pl.semaphore_wait(barrier, 33)

    def send_kv(i, carry):
        target = lax.rem(me + i, 32)
        to_ctx, to_y = target // 2, lax.rem(target, 2)
        columns = pl.ds(pl.multiple_of(to_ctx // 2 * HD, HD), HD)
        for_core(
            lax.rem(to_ctx, 2),
            lambda source: pltpu.make_async_remote_copy(
                src_ref=source.at[:, columns], dst_ref=raw.at[me],
                send_sem=kv_send, recv_sem=kv_recv,
                device_id=(to_ctx, to_y * PLANES + z), device_id_type=MESH,
            ).start(),
        )
        return carry

    lax.fori_loop(1, 32, send_kv, 0)

    def send_q(i, carry):
        target = lax.rem(me + i, 32)
        to_ctx, to_y = target // 2, lax.rem(target, 2)
        columns = pl.ds(pl.multiple_of(to_ctx // 2 * WIDE, HD), WIDE)
        pltpu.make_async_remote_copy(
            src_ref=q_in.at[2 * to_y + lax.rem(to_ctx, 2), :, columns],
            dst_ref=q_buf.at[me],
            send_sem=q_send,
            recv_sem=q_recv,
            device_id=(to_ctx, to_y * PLANES + z),
            device_id_type=MESH,
        ).start()
        return carry

    lax.fori_loop(1, 32, send_q, 0)

    def ring(distance, upward):
        if upward:
            chunk, device, sems = lax.rem(z + PLANES - (distance - 1), PLANES), above, (up_send, up_recv)
        else:
            chunk, device, sems = lax.rem(z + distance - 1, PLANES), below, (down_send, down_recv)
        whole = kv.at[chunk, core]
        if distance == 4:
            whole = whole.at[pl.ds(0 if upward else CHUNK // 2, CHUNK // 2)]
        return pltpu.make_async_remote_copy(
            src_ref=whole, dst_ref=whole,
            send_sem=sems[0].at[distance - 1], recv_sem=sems[1].at[distance - 1],
            device_id=device, device_id_type=MESH,
        )

    def across(step, chunk):
        return pltpu.make_async_remote_copy(
            src_ref=kv.at[chunk, core], dst_ref=kv.at[chunk, core],
            send_sem=near_send.at[step], recv_sem=near_recv.at[step],
            device_id=sibling, device_id_type=MESH,
        )

    for t, (first, last) in enumerate(SPAN):
        shape = (last - first, TILE)
        row = lax.broadcasted_iota(jnp.int32, shape, 0) + first
        column = lax.broadcasted_iota(jnp.int32, shape, 1) + t * TILE
        key_block, query_block = row // PART, column // QROWS
        key_row, query_row = lax.rem(row, PART), lax.rem(column, ROWS)
        mine = z * PART + part * ROWS + query_row
        for kind, (key_at, query_at) in enumerate(
            ((0, 0), (z * PART + key_row, mine), (1, 0))
        ):
            kept = key_block * BLK + key_at <= query_block * BLK + query_at
            bias[kind, t, : last - first, :] = jnp.where(kept, 0.0, LOW)
    ones[...] = jnp.ones_like(ones)
    acc[...] = jnp.zeros_like(acc)
    top[...] = jnp.full_like(top, LOW)

    pltpu.make_async_copy(raw.at[0], raw.at[0], kv_own).wait()
    many = raw.at[pl.ds(0, 31)]
    pltpu.make_async_copy(many, many, kv_recv).wait()
    for p in range(0, BLOCKS, 4):
        rows = jnp.concatenate([raw[block_at[p + i]] for i in range(4)], axis=0)

        @pl.when(core == 0)
        def _():
            kv[z, 0, p * PART : (p + 4) * PART, :] = rows

        @pl.when(core == 1)
        def _():
            kv[z, 1, p * PART : (p + 4) * PART, :] = rows.T

    ring(1, True).start()
    ring(1, False).start()
    across(0, z).start()

    own_q.wait()
    many_q = q_buf.at[pl.ds(0, 31)]
    pltpu.make_async_copy(many_q, many_q, q_recv).wait()

    def heads_as_rows(block):
        return jnp.concatenate([block[:, j * HD : (j + 1) * HD] for j in range(GROUP)], axis=0)

    for p in range(0, BLOCKS, 2):
        pair = [heads_as_rows(q_buf[block_at[p + i]]) for i in range(2)]
        qs[p * QROWS : (p + 2) * QROWS, :] = jnp.concatenate(pair, axis=0)

    def one_chunk(step, carry):
        distance = (step + 1) // 2
        from_below = lax.rem(step, 2) == 1
        chunk = lax.rem(jnp.where(from_below, z + PLANES - distance, z + distance), PLANES)
        for d in range(1, 5):

            @pl.when(step == 2 * d - 1)
            def _():
                ring(d, True).wait_recv()
                ring(d, False).wait_recv()
                if d < 4:
                    ring(d + 1, True).start()
                    ring(d + 1, False).start()
                    across(2 * d - 1, lax.rem(z + PLANES - d, PLANES)).start()
                    across(2 * d, lax.rem(z + d, PLANES)).start()
                else:
                    across(7, lax.rem(z + 4, PLANES)).start()

        other = kv.at[chunk, 1 - core]
        pltpu.make_async_copy(other, other, near_recv.at[step]).wait()

        kind = jnp.where(chunk < z, 0, jnp.where(chunk == z, 1, 2))
        def scores(t):
            return lax.dot_general(
                kv[chunk, 0, : SPAN[t][1], :], qs[t * TILE : (t + 1) * TILE, :],
                (((1,), (1,)), ((), ())), preferred_element_type=jnp.float32,
            )

        def weights(t, score):
            first, last = SPAN[t]
            edge = score[first:] + bias[kind, t, : last - first, :]
            score = jnp.concatenate([score[:first], edge], axis=0) if first else edge
            old = top[t]
            here = jnp.max(jnp.max(score.reshape(last // 8, 8, TILE), axis=0), axis=0, keepdims=True)
            new = jnp.maximum(old, jnp.broadcast_to(here, (8, TILE)))
            top[t] = new
            weight = jnp.exp2((score - new[0:1]) * SCALE).astype(jnp.bfloat16)
            return weight, jnp.exp2((old - new) * SCALE)

        def add(t, weight, factor):
            last = SPAN[t][1]
            values = [kv[chunk, 1, at : at + HD, : min(HD, last - at)] for at in range(0, last, HD)]
            columns = jnp.concatenate([jnp.concatenate(values, axis=1), ones[:, :last]], axis=0)
            mixed = jnp.dot(columns, weight, preferred_element_type=jnp.float32)
            acc[t] = acc[t] * factor[0:1] + mixed

        score, before = scores(0), None
        for t in range(TILES):
            following = scores(t + 1) if t + 1 < TILES else None
            current = (t,) + weights(t, score)
            if before is not None:
                add(*before)
            before, score = current, following
        add(*before)
        return carry

    lax.fori_loop(0, PLANES, one_chunk, 0)

    for t in range(TILES):
        total = acc[t]
        rows = (total[:HD] / total[HD : HD + 1]).T
        at = t * TILE
        while at < (t + 1) * TILE:
            block, row = at // QROWS, at % QROWS
            count = min(QROWS - row, (t + 1) * TILE - at)
            result[block, row : row + count, :] = rows[at - t * TILE : at - t * TILE + count]
            at += count

    def out_copy(b, device_rows):
        return out.at[device_rows, :, pl.ds(pl.multiple_of(g * WIDE, HD), WIDE)]

    def send_back(i, carry):
        b = lax.rem(me + i, BLOCKS)
        rows = result[order[b]].astype(jnp.bfloat16)
        o_buf[b] = jnp.concatenate([rows[j * ROWS : (j + 1) * ROWS] for j in range(GROUP)], axis=1)

        @pl.when(i < BLOCKS)
        def _():
            pltpu.make_async_remote_copy(
                src_ref=o_buf.at[b], dst_ref=out_copy(b, part),
                send_sem=o_send, recv_sem=o_recv,
                device_id=plane_device(b), device_id_type=MESH,
            ).start()

        return carry

    lax.fori_loop(1, BLOCKS + 1, send_back, 0)
    own_o = pltpu.make_async_copy(o_buf.at[me], out_copy(me, part), o_own)
    own_o.start()

    many_o = o_buf.at[pl.ds(0, 31)]
    pltpu.make_async_copy(many_q, many_q, q_send).wait()
    pltpu.make_async_copy(many, many, kv_send).wait()
    for d in range(1, 5):
        ring(d, True).wait_send()
        ring(d, False).wait_send()
    for step in range(PLANES):
        across(step, z).wait_send()
    own_o.wait()
    pltpu.make_async_copy(many_o, many_o, o_send).wait()
    pltpu.make_async_copy(many_o, many_o, o_recv).wait()


def shards(queries, keys, values, order):
    stored = jnp.arange(BLOCKS, dtype=jnp.int32)
    block_at = jnp.sum(jnp.where(order[None, :] == stored[:, None], stored[None, :], 0), axis=1)
    hbm = pl.BlockSpec(memory_space=pl.ANY)
    dma = pltpu.SemaphoreType.DMA
    out = pl.pallas_call(
        kernel,
        out_shape=jax.ShapeDtypeStruct((PART // ROWS, ROWS, 8 * WIDE), jnp.bfloat16),
        in_specs=[pl.BlockSpec(memory_space=pltpu.SMEM)] * 2 + [hbm, hbm, hbm],
        out_specs=hbm,
        scratch_shapes=[
            pltpu.VMEM((BLOCKS, ROWS, WIDE), jnp.bfloat16),
            pltpu.VMEM((BLOCKS, PART, HD), jnp.bfloat16),
            pltpu.VMEM((PLANES, 2, CHUNK, HD), jnp.bfloat16),
            pltpu.VMEM((QALL, HD), jnp.bfloat16),
            pltpu.VMEM((VROWS - HD, CHUNK), jnp.bfloat16),
            pltpu.VMEM((TILES, VROWS, TILE), jnp.float32),
            pltpu.VMEM((TILES, 8, TILE), jnp.float32),
            pltpu.VMEM((3, TILES, EDGE, TILE), jnp.float32),
            pltpu.VMEM((BLOCKS, QROWS, HD), jnp.float32),
            pltpu.VMEM((BLOCKS, ROWS, WIDE), jnp.bfloat16),
            dma, dma, dma, dma, dma, dma,
            dma((4,)), dma((4,)), dma((4,)), dma((4,)), dma((8,)), dma((8,)),
            dma, dma, dma,
        ],
        compiler_params=pltpu.CompilerParams(
            collective_id=0, has_side_effects=True, vmem_limit_bytes=48 * 2**20
        ),
        cost_estimate=pl.CostEstimate(
            flops=4 * QALL * BLOCKS * BLK * HD // 2, bytes_accessed=2**21, transcendentals=QALL * 4096
        ),
    )(order, block_at, queries.reshape(PART // ROWS, ROWS, 8 * WIDE), keys, values)
    return out.reshape(PART, 8 * WIDE)


def solution(mesh):
    rows = P(("ctx", "head"), None)
    return jax.shard_map(
        shards, mesh=mesh, in_specs=(rows, rows, rows, P()), out_specs=rows, check_vma=False
    )
```

time: 334 us -> 63.6 us (0.19); the launches traced: 329 us -> 62.8 us
  waiting for transfers between devices: 118 us -> 0 us
  blocking collectives: 61.2 us -> 0 us
  Pallas kernels: 0 us -> 58.6 us
  matrix products: 57 us -> 0 us
  local copies, waits for them, and re-layouts: 31.3 us -> 4.12 us
  other arithmetic: 25.1 us -> 0.11 us
  loops' own time: 15.1 us -> 0 us
  between operations: 13.6 us -> 0.02 us
  starting transfers between devices: 7.08 us -> 0 us
    all_gather x2 -> x0, waiting for transfers between devices: 107 us -> none  [the longest x1 69 us: shards(): value_piece = lax.all_gather(local_values, 'ctx', axis=0, tiled=True)]
    all_to_all x3 -> x0, blocking collectives: 61.2 us -> none  [the longest x1 21.3 us: shards(): lax.all_to_all(arrange(key_heads), 'head', split_axis=0, concat_axis=1, t...]
    pallas_call x0 -> x1, Pallas kernels: none -> 58.6 us  [shards(): pl.pallas_call(kernel, out_shape=jax.ShapeDtypeStruct((PART // ROWS, ROWS...]
    dot_general x16 -> x0, matrix products: 57 us -> none  [the longest x8 34.6 us: update(): jnp.einsum('gjqk,kgjd->gjqd', weight.astype(jnp.bfloat16), value_four, pr...]
    while x3 -> x0, local copies, waits for them, and re-layouts: 17.4 us -> none  [shards(): lax.scan(one_step, initial, (key_steps, value_steps, jnp.arange(steps, dt...]
    reduce_sum x17 -> x1, other arithmetic: 15.5 us -> 0.11 us  [shards(): jnp.sum(jnp.where(order[None, :] == stored[:, None], stored[None, :], 0),...]
    another operation x9 -> x0, loops' own time: 15.1 us -> none  [the longest x1 14.7 us: shards(): lax.scan(one_step, initial, (key_steps, value_steps, jnp.arange(steps, dt...]
    all_to_all x1 -> x0, waiting for transfers between devices: 11.1 us -> none  [shards(): lax.all_to_all(outgoing, 'head', split_axis=0, concat_axis=1, tiled=True)]
  transfers between devices with their start and end apart: 3 -> 0, of which waited for: 3 -> 0; matrix products, arithmetic and copies ran while one was open for 4% -> 0% of each run, Pallas kernels for 0% -> 0%
where the time goes in v1:
time: 63.6 us; the launch traced here: 62.8 us
  Pallas kernels  58.6 us (92%)
  local copies, waits for them, and re-layouts  4.12 us (6%)
    pallas_call x1, Pallas kernels, shards(): pl.pallas_call(kernel, out_shape=jax.ShapeDtypeStruct((PART // ROWS, ROWS...  58.6 us
    unnamed x9, local copies, waits for them, and re-layouts  4.12 us

profile of v1, /device:TPU:25, one launch (start us, length us, event | category | flops | bytes accessed | tf_op | source)
XLA Modules:
  0.0 62.8 jit_solution(11330637337206873204)
XLA Ops:
  0.0 0.0 copy-start.3
  0.0 0.7 %copy-done.3 = s32[32]{0:T(128)S(1)} copy-done((s32[32]{0:T(128)S(1)}, s32[32]{0:T(128)}, u32[]{:S(2)}) %copy-start.3) | copy-done | bytes 152
  0.7 0.1 select_reduce_fusion.block_at
  0.8 0.0 copy-start
  0.8 1.0 %copy-done = bf16[32,7168]{1,0:T(8,128)(2,1)S(1)} copy-done((bf16[32,7168]{1,0:T(8,128)(2,1)S(1)}, bf16[32,7168]{1,0:T(8,128)(2,1)}, u32[]{:S(2)}) %copy-start) | copy-done | bytes 458776
  1.8 0.0 copy-start.1
  1.8 0.8 %copy-done.1 = bf16[32,1024]{1,0:T(8,128)(2,1)S(1)} copy-done((bf16[32,1024]{1,0:T(8,128)(2,1)S(1)}, bf16[32,1024]{1,0:T(8,128)(2,1)}, u32[]{:S(2)}) %copy-start.1) | copy-done | bytes 65560
  2.6 0.0 copy-start.2
  2.6 0.8 %copy-done.2 = bf16[32,1024]{1,0:T(8,128)(2,1)S(1)} copy-done((bf16[32,1024]{1,0:T(8,128)(2,1)S(1)}, bf16[32,1024]{1,0:T(8,128)(2,1)}, u32[]{:S(2)}) %copy-start.2) | copy-done | bytes 65560
  3.5 58.6 %shard_map.46 = bf16[4,8,7168]{2,1,0:T(8,128)(2,1)S(1)} custom-call(s32[32]{0:T(128)S(1)} %copy-done.3, s32[32]{0:T(128)S(1)} %select_reduce_fusion.block_at, bf16[4,8,7168]{2,1,0:T(8,128)(2,1)S(1)} %bitcast.3, bf16[32,1024]{1,0:T(8,128)(2,1)S(1)} %copy-done.1, bf16[32,1024]{1,0:T(8,128)(2,1)S(1)} %copy-done.2), custom_call_target="tpu_custom_call" | custom-call | flops 3758096384 | bytes 2097152 | tf_op jit(solution)/shard_map/pallas_call | solution.py:288
  62.1 0.8 %copy.6 = bf16[32,7168]{1,0:T(8,128)(2,1)} copy(bf16[32,7168]{1,0:T(8,128)(2,1)S(1)} %bitcast.2) | data formatting | bytes 917504
Async XLA Ops:
  0.0 0.7 %copy-start.3 = (s32[32]{0:T(128)S(1)}, s32[32]{0:T(128)}, u32[]{:S(2)}) copy-start(s32[32]{0:T(128)} %order.1) | copy-start | bytes 388
  0.8 1.0 %copy-start = (bf16[32,7168]{1,0:T(8,128)(2,1)S(1)}, bf16[32,7168]{1,0:T(8,128)(2,1)}, u32[]{:S(2)}) copy-start(bf16[32,7168]{1,0:T(8,128)(2,1)} %param.4) | copy-start | bytes 1376260
  1.8 0.8 %copy-start.1 = (bf16[32,1024]{1,0:T(8,128)(2,1)S(1)}, bf16[32,1024]{1,0:T(8,128)(2,1)}, u32[]{:S(2)}) copy-start(bf16[32,1024]{1,0:T(8,128)(2,1)} %k_in.1) | copy-start | bytes 196612
  2.6 0.8 %copy-start.2 = (bf16[32,1024]{1,0:T(8,128)(2,1)S(1)}, bf16[32,1024]{1,0:T(8,128)(2,1)}, u32[]{:S(2)}) copy-start(bf16[32,1024]{1,0:T(8,128)(2,1)} %v_in.1) | copy-start | bytes 196612

commit v2 on v1

v2 whole, which is shorter than its diff:
```python
import jax
import jax.numpy as jnp
from jax import lax
from jax.experimental import pallas as pl
from jax.experimental.pallas import tpu as pltpu
from jax.sharding import PartitionSpec as P

MESH = pl.DeviceIdType.MESH
HD = 128
GROUP = 7
PLANES = 8
BLOCKS = 32
PART = 32
ROWS = 8
BLK = 256
QROWS = GROUP * ROWS
QALL = BLOCKS * QROWS
CHUNK = BLOCKS * PART
WIDE = GROUP * HD
TILE = 256
TILES = QALL // TILE
VROWS = HD + 16
SCALE = HD**-0.5 * 1.4426950408889634
MASKED = -1e30

SPAN = [
    ((TILE * t) // QROWS * PART, ((TILE * t + TILE - 1) // QROWS + 1) * PART) for t in range(TILES)
]
EDGE = max(last - first for first, last in SPAN)

PIECES = 4
PIECE = CHUNK // PIECES
UP, DOWN = (0, 1, 2, 3), (1, 0, 3, 2)
HALF = CHUNK // 2
LOW = [(t, 0, min(HALF, last)) for t, (first, last) in enumerate(SPAN)]
HIGH = [(t, HALF, last) for t, (first, last) in enumerate(SPAN) if last > HALF]


def kernel(
    order, q_in, k_in, v_in, out,
    q_held, kv_in, kv_held, q_buf, raw, kv, qs, ones, acc, top, bias, result, o_buf, block_at,
    fetch, q_send, q_recv, q_own, kv_send, kv_recv, kv_own,
    up_send, up_recv, down_send, down_recv, near_send, near_recv,
    o_send, o_recv, o_own,
):
    ctx = lax.axis_index("ctx")
    head = lax.axis_index("head")
    z = lax.rem(head, PLANES)
    y_lo = head // PLANES
    core = lax.rem(ctx, 2)
    g = ctx // 2
    part = 2 * y_lo + core
    me = 2 * ctx + y_lo
    sibling = (ctx + 1 - 2 * core, head)
    above = (ctx, y_lo * PLANES + lax.rem(z + 1, PLANES))
    below = (ctx, y_lo * PLANES + lax.rem(z + PLANES - 1, PLANES))

    def plane_device(index):
        return (index // 2, lax.rem(index, 2) * PLANES + z)

    fetches = [
        pltpu.make_async_copy(k_in, kv_in.at[0], fetch.at[0]),
        pltpu.make_async_copy(v_in, kv_in.at[1], fetch.at[1]),
        pltpu.make_async_copy(q_in, q_held, fetch.at[2]),
    ]
    for copy in fetches:
        copy.start()

    barrier = pltpu.get_barrier_semaphore()

    def greet(i, carry):
        pl.semaphore_signal(
            barrier, inc=1, device_id=plane_device(lax.rem(me + i, 32)), device_id_type=MESH
        )
        return carry

    lax.fori_loop(1, 32, greet, 0)
    for device in (above, below):
        pl.semaphore_signal(barrier, inc=1, device_id=device, device_id_type=MESH)

    fetches[0].wait()
    fetches[1].wait()
    for which in range(2):
        for to_g in range(8):
            kv_held[which, to_g] = kv_in[which, :, to_g * HD : (to_g + 1) * HD]
    own_kv = pltpu.make_async_copy(kv_held.at[core, g], raw.at[me], kv_own)
    own_kv.start()

    pl.semaphore_wait(barrier, 33)

    def send_kv(i, carry):
        target = lax.rem(me + i, 32)
        to_ctx, to_y = target // 2, lax.rem(target, 2)
        pltpu.make_async_remote_copy(
            src_ref=kv_held.at[lax.rem(to_ctx, 2), to_ctx // 2], dst_ref=raw.at[me],
            send_sem=kv_send, recv_sem=kv_recv,
            device_id=(to_ctx, to_y * PLANES + z), device_id_type=MESH,
        ).start()
        return carry

    lax.fori_loop(1, 32, send_kv, 0)

    fetches[2].wait()
    own_q = pltpu.make_async_copy(
        q_held.at[part, :, pl.ds(pl.multiple_of(g * WIDE, HD), WIDE)], q_buf.at[me], q_own
    )
    own_q.start()

    def send_q(i, carry):
        target = lax.rem(me + i, 32)
        to_ctx, to_y = target // 2, lax.rem(target, 2)
        columns = pl.ds(pl.multiple_of(to_ctx // 2 * WIDE, HD), WIDE)
        pltpu.make_async_remote_copy(
            src_ref=q_held.at[2 * to_y + lax.rem(to_ctx, 2), :, columns],
            dst_ref=q_buf.at[me],
            send_sem=q_send,
            recv_sem=q_recv,
            device_id=(to_ctx, to_y * PLANES + z),
            device_id_type=MESH,
        ).start()
        return carry

    lax.fori_loop(1, 32, send_q, 0)

    def ring(distance, upward, turn):
        if upward:
            chunk, device, sems = lax.rem(z + PLANES + 1 - distance, PLANES), above, (up_send, up_recv)
        else:
            chunk, device, sems = lax.rem(z + distance - 1, PLANES), below, (down_send, down_recv)
        held = kv.at[chunk, core, pl.ds((UP if upward else DOWN)[turn] * PIECE, PIECE)]
        index = (distance - 1) * PIECES + turn
        return pltpu.make_async_remote_copy(
            src_ref=held, dst_ref=held,
            send_sem=sems[0].at[index], recv_sem=sems[1].at[index],
            device_id=device, device_id_type=MESH,
        )

    def across(step, chunk, first, count=1):
        held = kv.at[chunk, core, pl.ds(first * PIECE, count * PIECE)]
        return pltpu.make_async_remote_copy(
            src_ref=held, dst_ref=held,
            send_sem=near_send.at[step], recv_sem=near_recv.at[step],
            device_id=sibling, device_id_type=MESH,
        )

    def pass_on(distance, turn):
        ring(distance, True, turn).wait_recv()
        ring(distance, False, turn).wait_recv()

        @pl.when((distance < 3) | (distance == 3) & (turn % 2 == 0))
        def _():
            ring(distance + 1, True, turn).start()
            ring(distance + 1, False, turn).start()

        step = 2 * distance + turn // 2
        across(step, lax.rem(z + PLANES - distance, PLANES), UP[turn]).start()
        across(step, lax.rem(z + distance, PLANES), DOWN[turn]).start()

    def from_sibling(step, count):
        held = kv.at[z, 1 - core, pl.ds(0, count * PIECE)]
        pltpu.make_async_copy(held, held, near_recv.at[step]).wait()

    for p in range(BLOCKS):
        at = jnp.int32(0)
        for b in range(BLOCKS):
            at = at + jnp.where(order[b] == p, b, 0)
        block_at[p] = jnp.minimum(at, BLOCKS - 1)
    for t, (first, last) in enumerate(SPAN):
        shape = (last - first, TILE)
        row = lax.broadcasted_iota(jnp.int32, shape, 0) + first
        column = lax.broadcasted_iota(jnp.int32, shape, 1) + t * TILE
        key_block, query_block = row // PART, column // QROWS
        key_row, query_row = lax.rem(row, PART), lax.rem(column, ROWS)
        mine = z * PART + part * ROWS + query_row
        for kind, (key_at, query_at) in enumerate(
            ((0, 0), (z * PART + key_row, mine), (1, 0))
        ):
            kept = key_block * BLK + key_at <= query_block * BLK + query_at
            bias[kind, t, : last - first, :] = jnp.where(kept, 0.0, MASKED)
    ones[...] = jnp.ones_like(ones)
    acc[...] = jnp.zeros_like(acc)
    top[...] = jnp.full_like(top, MASKED)

    own_kv.wait()
    many = raw.at[pl.ds(0, 31)]
    pltpu.make_async_copy(many, many, kv_recv).wait()
    def sort_piece(piece):
        for p in range(piece * 8, piece * 8 + 8, 4):
            rows = jnp.concatenate([raw[block_at[p + i]] for i in range(4)], axis=0)

            @pl.when(core == 0)
            def _():
                kv[z, 0, p * PART : (p + 4) * PART, :] = rows

            @pl.when(core == 1)
            def _():
                kv[z, 1, p * PART : (p + 4) * PART, :] = rows.T

        across(piece // 2, z, piece).start()

    sort_piece(0)
    ring(1, True, 0).start()
    sort_piece(1)
    ring(1, False, 0).start()
    ring(1, True, 1).start()
    ring(1, False, 1).start()
    sort_piece(2)
    ring(1, True, 2).start()
    sort_piece(3)
    ring(1, False, 2).start()
    ring(1, True, 3).start()
    ring(1, False, 3).start()

    pass_on(1, 0)
    from_sibling(0, 2)
    own_q.wait()
    many_q = q_buf.at[pl.ds(0, 31)]
    pltpu.make_async_copy(many_q, many_q, q_recv).wait()

    def heads_as_rows(block):
        return jnp.concatenate([block[:, j * HD : (j + 1) * HD] for j in range(GROUP)], axis=0)

    for p in range(0, BLOCKS, 2):
        pair = [heads_as_rows(q_buf[block_at[p + i]]) for i in range(2)]
        qs[p * QROWS : (p + 2) * QROWS, :] = jnp.concatenate(pair, axis=0)

    def attend(chunks, between):
        spans = LOW + HIGH
        kinds = [jnp.where(chunk < z, 0, jnp.where(chunk == z, 1, 2)) for chunk in chunks]

        def scores(span):
            t, begin, end = span
            held = [kv[chunk, 0, begin:end, :] for chunk in chunks]
            held = jnp.concatenate(held, axis=0) if len(held) > 1 else held[0]
            return lax.dot_general(
                held, qs[t * TILE : (t + 1) * TILE, :],
                (((1,), (1,)), ((), ())), preferred_element_type=jnp.float32,
            )

        def weights(span, score):
            t, begin, end = span
            edge = max(SPAN[t][0], begin)
            parts = []
            for i, kind in enumerate(kinds):
                part = score[i * (end - begin) : (i + 1) * (end - begin)]
                if edge >= end:
                    parts.append(part)
                    continue
                if edge > begin:
                    parts.append(part[: edge - begin])
                parts.append(part[edge - begin :] + bias[kind, t, edge - SPAN[t][0] : end - SPAN[t][0], :])
            score = jnp.concatenate(parts, axis=0) if len(parts) > 1 else parts[0]
            old = top[t]
            here = jnp.max(score.reshape(score.shape[0] // 8, 8, TILE), axis=0)
            here = jnp.max(here, axis=0, keepdims=True)
            new = jnp.maximum(old, jnp.broadcast_to(here, (8, TILE)))
            top[t] = new
            weight = jnp.exp2((score - new[0:1]) * SCALE).astype(jnp.bfloat16)
            return weight, jnp.exp2((old - new) * SCALE)

        def add(span, weight, factor):
            t, begin, end = span
            values = [
                kv[chunk, 1, at : at + HD, : min(HD, end - at)]
                for chunk in chunks for at in range(begin, end, HD)
            ]
            columns = jnp.concatenate(values, axis=1) if len(values) > 1 else values[0]
            columns = jnp.concatenate([columns, ones[:, : weight.shape[0]]], axis=0)
            acc[t] = acc[t] * factor[0:1] + jnp.dot(columns, weight, preferred_element_type=jnp.float32)

        score, before = scores(spans[0]), None
        for i, span in enumerate(spans):
            following = scores(spans[i + 1]) if i + 1 < len(spans) else None
            current = (span,) + weights(span, score)
            if before is not None:
                add(*before)
            before, score = current, following
            if i in between:
                between[i]()
        add(*before)

    def one_distance(distance, carry):
        lower, upper = lax.rem(z + PLANES - distance, PLANES), lax.rem(z + distance, PLANES)
        alone = (distance == 0) | (distance == 4)

        @pl.when(alone)
        def _():
            def late_first():
                pl.when(distance == 0)(lambda: pass_on(1, 1))

            def late_high():
                @pl.when(distance == 0)
                def _():
                    from_sibling(1, 2)

                @pl.when(distance == 4)
                def _():
                    pass_on(4, 2)
                    from_sibling(9, 2)

            attend((upper,), {1: late_first, len(LOW) - 2: late_high})
            pl.when(distance == 0)(lambda: from_sibling(2, 4))

        @pl.when(jnp.logical_not(alone))
        def _():
            def last_piece():
                pass_on(distance, 3)
                from_sibling(2 * distance + 1, 4)

            def next_second():
                pl.when(distance < 3)(lambda: pass_on(distance + 1, 1))

            attend(
                (lower, upper),
                {
                    2: lambda: pass_on(distance, 2),
                    len(LOW) - 2: last_piece,
                    len(LOW) + 1: lambda: pass_on(distance + 1, 0),
                    len(LOW) + 2: next_second,
                },
            )
            pl.when(distance < 3)(lambda: from_sibling(2 * distance + 2, 4))
            pl.when(distance == 3)(lambda: from_sibling(8, 2))

        return carry

    lax.fori_loop(0, 5, one_distance, 0)

    for t in range(TILES):
        total = acc[t]
        rows = (total[:HD] / total[HD : HD + 1]).T
        at = t * TILE
        while at < (t + 1) * TILE:
            block, row = at // QROWS, at % QROWS
            count = min(QROWS - row, (t + 1) * TILE - at)
            result[block, row : row + count, :] = rows[at - t * TILE : at - t * TILE + count]
            at += count

    def out_copy(b, device_rows):
        return out.at[device_rows, :, pl.ds(pl.multiple_of(g * WIDE, HD), WIDE)]

    def send_back(i, carry):
        b = lax.rem(me + i, BLOCKS)
        rows = result[order[b]].astype(jnp.bfloat16)
        o_buf[b] = jnp.concatenate([rows[j * ROWS : (j + 1) * ROWS] for j in range(GROUP)], axis=1)

        @pl.when(i < BLOCKS)
        def _():
            pltpu.make_async_remote_copy(
                src_ref=o_buf.at[b], dst_ref=out_copy(b, part),
                send_sem=o_send, recv_sem=o_recv,
                device_id=plane_device(b), device_id_type=MESH,
            ).start()

        return carry

    lax.fori_loop(1, BLOCKS + 1, send_back, 0)
    own_o = pltpu.make_async_copy(o_buf.at[me], out_copy(me, part), o_own)
    own_o.start()

    many_o = o_buf.at[pl.ds(0, 31)]
    pltpu.make_async_copy(many_q, many_q, q_send).wait()
    pltpu.make_async_copy(many, many, kv_send).wait()
    for distance in range(1, 5):
        for turn in range(0, PIECES, 1 if distance < 4 else 2):
            ring(distance, True, turn).wait_send()
            ring(distance, False, turn).wait_send()
    for step in range(10):
        across(step, z, 0, 4 if 2 <= step < 8 else 2).wait_send()
    own_o.wait()
    pltpu.make_async_copy(many_o, many_o, o_send).wait()
    pltpu.make_async_copy(many_o, many_o, o_recv).wait()


def shards(queries, keys, values, order):
    hbm = pl.BlockSpec(memory_space=pltpu.HBM)
    dma = pltpu.SemaphoreType.DMA
    out = pl.pallas_call(
        kernel,
        out_shape=pltpu.VMEM((PART // ROWS, ROWS, 8 * WIDE), jnp.bfloat16),
        in_specs=[pl.BlockSpec(memory_space=pltpu.SMEM), hbm, hbm, hbm],
        out_specs=pl.BlockSpec(memory_space=pltpu.VMEM),
        scratch_shapes=[
            pltpu.VMEM((PART // ROWS, ROWS, 8 * WIDE), jnp.bfloat16),
            pltpu.VMEM((2, PART, 8 * HD), jnp.bfloat16),
            pltpu.VMEM((2, 8, PART, HD), jnp.bfloat16),
            pltpu.VMEM((BLOCKS, ROWS, WIDE), jnp.bfloat16),
            pltpu.VMEM((BLOCKS, PART, HD), jnp.bfloat16),
            pltpu.VMEM((PLANES, 2, CHUNK, HD), jnp.bfloat16),
            pltpu.VMEM((QALL, HD), jnp.bfloat16),
            pltpu.VMEM((VROWS - HD, CHUNK), jnp.bfloat16),
            pltpu.VMEM((TILES, VROWS, TILE), jnp.float32),
            pltpu.VMEM((TILES, 8, TILE), jnp.float32),
            pltpu.VMEM((3, TILES, EDGE, TILE), jnp.float32),
            pltpu.VMEM((BLOCKS, QROWS, HD), jnp.float32),
            pltpu.VMEM((BLOCKS, ROWS, WIDE), jnp.bfloat16),
            pltpu.SMEM((BLOCKS,), jnp.int32),
            dma((3,)), dma, dma, dma, dma, dma, dma,
            *[dma((4 * PIECES,))] * 4, dma((10,)), dma((10,)),
            dma, dma, dma,
        ],
        compiler_params=pltpu.CompilerParams(
            collective_id=0, has_side_effects=True, vmem_limit_bytes=60 * 2**20
        ),
        cost_estimate=pl.CostEstimate(
            flops=4 * QALL * BLOCKS * BLK * HD // 2, bytes_accessed=2**21, transcendentals=QALL * 4096
        ),
    )(order, queries.reshape(PART // ROWS, ROWS, 8 * WIDE), keys, values)
    return out.reshape(PART, 8 * WIDE)


def solution(mesh):
    rows = P(("ctx", "head"), None)
    return jax.shard_map(
        shards, mesh=mesh, in_specs=(rows, rows, rows, P()), out_specs=rows, check_vma=False
    )
```

time: 63.6 us -> 55.1 us (0.87)
  Pallas kernels: 58.6 us -> 54.1 us
  local copies, waits for them, and re-layouts: 4.12 us -> 0.77 us
    pallas_call x1, Pallas kernels: 58.6 us -> 54.1 us  [shards(): pl.pallas_call(kernel, out_shape=pltpu.VMEM((PART // ROWS, ROWS, 8 * WIDE...]
    unnamed x9 -> x1, local copies, waits for them, and re-layouts: 4.12 us -> 0.77 us
where the time goes in v2:
time: 55.1 us; the launch traced here: 54.9 us
  Pallas kernels  54.1 us (98%)
  local copies, waits for them, and re-layouts  0.77 us (1%)
    pallas_call x1, Pallas kernels, shards(): pl.pallas_call(kernel, out_shape=pltpu.VMEM((PART // ROWS, ROWS, 8 * WIDE...  54.1 us

profile of v2, /device:TPU:25, one launch (start us, length us, event | category | flops | bytes accessed | tf_op | source)
XLA Modules:
  0.0 54.9 jit_solution(1550175997486037950)
XLA Ops:
  0.0 54.1 %shard_map.46 = bf16[4,8,7168]{2,1,0:T(8,128)(2,1)S(1)} custom-call(s32[32]{0:T(128)} %order.1, bf16[4,8,7168]{2,1,0:T(8,128)(2,1)} %bitcast.3, bf16[32,1024]{1,0:T(8,128)(2,1)} %k_in.1, bf16[32,1024]{1,0:T(8,128)(2,1)} %v_in.1), custom_call_target="tpu_custom_call" | custom-call | flops 3758096384 | bytes 2097152 | tf_op jit(solution)/shard_map/pallas_call | solution.py:378
  54.1 0.8 %copy.6 = bf16[32,7168]{1,0:T(8,128)(2,1)} copy(bf16[32,7168]{1,0:T(8,128)(2,1)S(1)} %bitcast.2) | data formatting | bytes 917504

commit v3 on v2

--- a/solution.py
+++ b/solution.py
@@ -30,17 +30,32 @@
 
 PIECES = 4
 PIECE = CHUNK // PIECES
-UP, DOWN = (0, 1, 2, 3), (1, 0, 3, 2)
+TURNS = 3
 HALF = CHUNK // 2
-LOW = [(t, 0, min(HALF, last)) for t, (first, last) in enumerate(SPAN)]
-HIGH = [(t, HALF, last) for t, (first, last) in enumerate(SPAN) if last > HALF]
+
+
+def steps(*parts):
+    met = [
+        (t, tuple((chunk, begin, min(end, last)) for chunk, begin, end in parts if last > begin))
+        for t, (first, last) in enumerate(SPAN)
+    ]
+    met = [step for step in met if step[1]]
+    return met[0::2] + met[1::2][::-1]
+
+
+def low(*chunks):
+    return steps(*[(chunk, 0, HALF) for chunk in chunks])
+
+
+def high(*chunks):
+    return steps(*[(chunk, HALF, CHUNK) for chunk in chunks])
 
 
 def kernel(
     order, q_in, k_in, v_in, out,
     q_held, kv_in, kv_held, q_buf, raw, kv, qs, ones, acc, top, bias, result, o_buf, block_at,
     fetch, q_send, q_recv, q_own, kv_send, kv_recv, kv_own,
-    up_send, up_recv, down_send, down_recv, near_send, near_recv,
+    up_send, up_recv, down_send, down_recv, near_send, near_recv, over_send, over_recv,
     o_send, o_recv, o_own,
 ):
     ctx = lax.axis_index("ctx")
@@ -122,13 +137,18 @@
 
     lax.fori_loop(1, 32, send_q, 0)
 
+    def piece_of(upward, turn):
+        if turn < 2:
+            return turn if upward else 1 - turn
+        return 2 + y_lo if upward else 3 - y_lo
+
     def ring(distance, upward, turn):
         if upward:
             chunk, device, sems = lax.rem(z + PLANES + 1 - distance, PLANES), above, (up_send, up_recv)
         else:
             chunk, device, sems = lax.rem(z + distance - 1, PLANES), below, (down_send, down_recv)
-        held = kv.at[chunk, core, pl.ds((UP if upward else DOWN)[turn] * PIECE, PIECE)]
-        index = (distance - 1) * PIECES + turn
+        held = kv.at[chunk, core, pl.ds(piece_of(upward, turn) * PIECE, PIECE)]
+        index = (distance - 1) * TURNS + turn
         return pltpu.make_async_remote_copy(
             src_ref=held, dst_ref=held,
             send_sem=sems[0].at[index], recv_sem=sems[1].at[index],
@@ -147,14 +167,38 @@
         ring(distance, True, turn).wait_recv()
         ring(distance, False, turn).wait_recv()
 
-        @pl.when((distance < 3) | (distance == 3) & (turn % 2 == 0))
+        @pl.when((distance < 3) | (distance == 3) & (turn != 1))
         def _():
             ring(distance + 1, True, turn).start()
             ring(distance + 1, False, turn).start()
 
+        lower, upper = lax.rem(z + PLANES - distance, PLANES), lax.rem(z + distance, PLANES)
+        if turn == 2:
+
+            @pl.when(distance < 4)
+            def _():
+                for chunk, upward in ((lower, True), (upper, False)):
+                    over(distance, chunk, piece_of(upward, 2)).start()
+
         step = 2 * distance + turn // 2
-        across(step, lax.rem(z + PLANES - distance, PLANES), UP[turn]).start()
-        across(step, lax.rem(z + distance, PLANES), DOWN[turn]).start()
+        if turn == 0:
+            step = jnp.where(distance == 3, 10, step)
+        across(step, lower, piece_of(True, turn)).start()
+        across(step, upper, piece_of(False, turn)).start()
+
+    def over(distance, chunk, first, count=1):
+        held = kv.at[chunk, core, pl.ds(first * PIECE, count * PIECE)]
+        return pltpu.make_async_remote_copy(
+            src_ref=held, dst_ref=held,
+            send_sem=over_send.at[distance - 1], recv_sem=over_recv.at[distance - 1],
+            device_id=(ctx, (1 - y_lo) * PLANES + z), device_id_type=MESH,
+        )
+
+    def take_over(distance):
+        over(distance, z, 0, 2).wait_recv()
+        step = 2 * distance + 1
+        across(step, lax.rem(z + PLANES - distance, PLANES), 3 - y_lo).start()
+        across(step, lax.rem(z + distance, PLANES), 2 + y_lo).start()
 
     def from_sibling(step, count):
         held = kv.at[z, 1 - core, pl.ds(0, count * PIECE)]
@@ -205,11 +249,9 @@
     ring(1, True, 1).start()
     ring(1, False, 1).start()
     sort_piece(2)
+    sort_piece(3)
     ring(1, True, 2).start()
-    sort_piece(3)
     ring(1, False, 2).start()
-    ring(1, True, 3).start()
-    ring(1, False, 3).start()
 
     pass_on(1, 0)
     from_sibling(0, 2)
@@ -224,32 +266,30 @@
         pair = [heads_as_rows(q_buf[block_at[p + i]]) for i in range(2)]
         qs[p * QROWS : (p + 2) * QROWS, :] = jnp.concatenate(pair, axis=0)
 
-    def attend(chunks, between):
-        spans = LOW + HIGH
-        kinds = [jnp.where(chunk < z, 0, jnp.where(chunk == z, 1, 2)) for chunk in chunks]
-
-        def scores(span):
-            t, begin, end = span
-            held = [kv[chunk, 0, begin:end, :] for chunk in chunks]
+    def attend(steps, between={}):
+        def scores(step):
+            t, parts = step
+            held = [kv[chunk, 0, begin:end, :] for chunk, begin, end in parts]
             held = jnp.concatenate(held, axis=0) if len(held) > 1 else held[0]
             return lax.dot_general(
                 held, qs[t * TILE : (t + 1) * TILE, :],
                 (((1,), (1,)), ((), ())), preferred_element_type=jnp.float32,
             )
 
-        def weights(span, score):
-            t, begin, end = span
-            edge = max(SPAN[t][0], begin)
-            parts = []
-            for i, kind in enumerate(kinds):
-                part = score[i * (end - begin) : (i + 1) * (end - begin)]
-                if edge >= end:
-                    parts.append(part)
-                    continue
+        def weights(step, score):
+            t, parts = step
+            biased, at = [], 0
+            for chunk, begin, end in parts:
+                kind = jnp.where(chunk < z, 0, jnp.where(chunk == z, 1, 2))
+                edge = min(max(SPAN[t][0], begin), end)
+                part = score[at : at + end - begin]
+                at += end - begin
                 if edge > begin:
-                    parts.append(part[: edge - begin])
-                parts.append(part[edge - begin :] + bias[kind, t, edge - SPAN[t][0] : end - SPAN[t][0], :])
-            score = jnp.concatenate(parts, axis=0) if len(parts) > 1 else parts[0]
+                    biased.append(part[: edge - begin])
+                if edge < end:
+                    rows = slice(edge - SPAN[t][0], end - SPAN[t][0])
+                    biased.append(part[edge - begin :] + bias[kind, t, rows, :])
+            score = jnp.concatenate(biased, axis=0) if len(biased) > 1 else biased[0]
             old = top[t]
             here = jnp.max(score.reshape(score.shape[0] // 8, 8, TILE), axis=0)
             here = jnp.max(here, axis=0, keepdims=True)
@@ -258,20 +298,20 @@
             weight = jnp.exp2((score - new[0:1]) * SCALE).astype(jnp.bfloat16)
             return weight, jnp.exp2((old - new) * SCALE)
 
-        def add(span, weight, factor):
-            t, begin, end = span
+        def add(step, weight, factor):
+            t, parts = step
             values = [
                 kv[chunk, 1, at : at + HD, : min(HD, end - at)]
-                for chunk in chunks for at in range(begin, end, HD)
+                for chunk, begin, end in parts for at in range(begin, end, HD)
             ]
             columns = jnp.concatenate(values, axis=1) if len(values) > 1 else values[0]
             columns = jnp.concatenate([columns, ones[:, : weight.shape[0]]], axis=0)
             acc[t] = acc[t] * factor[0:1] + jnp.dot(columns, weight, preferred_element_type=jnp.float32)
 
-        score, before = scores(spans[0]), None
-        for i, span in enumerate(spans):
-            following = scores(spans[i + 1]) if i + 1 < len(spans) else None
-            current = (span,) + weights(span, score)
+        score, before = scores(steps[0]), None
+        for i, step in enumerate(steps):
+            following = scores(steps[i + 1]) if i + 1 < len(steps) else None
+            current = (step,) + weights(step, score)
             if before is not None:
                 add(*before)
             before, score = current, following
@@ -288,6 +328,12 @@
             def late_first():
                 pl.when(distance == 0)(lambda: pass_on(1, 1))
 
+            def take_third():
+                pl.when(distance == 4)(lambda: take_over(3))
+
+            def last_first():
+                pl.when(distance == 0)(lambda: pass_on(1, 2))
+
             def late_high():
                 @pl.when(distance == 0)
                 def _():
@@ -298,28 +344,44 @@
                     pass_on(4, 2)
                     from_sibling(9, 2)
 
-            attend((upper,), {1: late_first, len(LOW) - 2: late_high})
-            pl.when(distance == 0)(lambda: from_sibling(2, 4))
-
-        @pl.when(jnp.logical_not(alone))
+            attend(low(upper) + high(upper), {1: late_first, TILES - 3: late_high, TILES: last_first, TILES - 1: take_third})
+
+        @pl.when((distance == 1) | (distance == 2))
         def _():
-            def last_piece():
-                pass_on(distance, 3)
-                from_sibling(2 * distance + 1, 4)
-
-            def next_second():
-                pl.when(distance < 3)(lambda: pass_on(distance + 1, 1))
-
+            def amid():
+                pl.when(distance == 1)(lambda: pass_on(2, 0))
+                pl.when(distance == 2)(lambda: pass_on(2, 2))
+
+            def late():
+                pl.when(distance == 2)(lambda: take_over(1))
+
+            def last():
+                pl.when(distance == 1)(lambda: pass_on(2, 1))
+                pl.when(distance == 2)(lambda: pass_on(3, 0))
+
+            from_sibling(2 * distance, 4)
+            attend(low(lower, upper), {0: amid, 2: late, 3: last})
+
+        @pl.when(distance == 3)
+        def _():
+            from_sibling(10, 2)
+            so_far = steps((lower, 0, PIECE), (upper, PIECE, HALF))
+            rest = steps((lower, PIECE, HALF), (upper, 0, PIECE))
             attend(
-                (lower, upper),
+                so_far + rest,
                 {
-                    2: lambda: pass_on(distance, 2),
-                    len(LOW) - 2: last_piece,
-                    len(LOW) + 1: lambda: pass_on(distance + 1, 0),
-                    len(LOW) + 2: next_second,
+                    0: lambda: pass_on(3, 1),
+                    TILES - 2: lambda: from_sibling(6, 2),
+                    TILES - 1: lambda: pass_on(3, 2),
+                    TILES + 1: lambda: take_over(2),
+                    TILES + 2: lambda: pass_on(4, 0),
                 },
             )
-            pl.when(distance < 3)(lambda: from_sibling(2 * distance + 2, 4))
+
+        @pl.when(distance > 1)
+        def _():
+            from_sibling(2 * distance - 1, 4)
+            attend(high(lax.rem(lower + 1, PLANES), lax.rem(upper + PLANES - 1, PLANES)))
             pl.when(distance == 3)(lambda: from_sibling(8, 2))
 
         return carry
@@ -328,7 +390,7 @@
 
     for t in range(TILES):
         total = acc[t]
-        rows = (total[:HD] / total[HD : HD + 1]).T
+        rows = (total[:HD] * (1.0 / total[HD : HD + 1])).T
         at = t * TILE
         while at < (t + 1) * TILE:
             block, row = at // QROWS, at % QROWS
@@ -339,22 +401,25 @@
     def out_copy(b, device_rows):
         return out.at[device_rows, :, pl.ds(pl.multiple_of(g * WIDE, HD), WIDE)]
 
-    def send_back(i, carry):
-        b = lax.rem(me + i, BLOCKS)
-        rows = result[order[b]].astype(jnp.bfloat16)
-        o_buf[b] = jnp.concatenate([rows[j * ROWS : (j + 1) * ROWS] for j in range(GROUP)], axis=1)
-
-        @pl.when(i < BLOCKS)
-        def _():
-            pltpu.make_async_remote_copy(
-                src_ref=o_buf.at[b], dst_ref=out_copy(b, part),
-                send_sem=o_send, recv_sem=o_recv,
-                device_id=plane_device(b), device_id_type=MESH,
-            ).start()
+    def send_back(group, carry):
+        indices = [4 * group + 1 + j for j in range(4)]
+        blocks = [lax.rem(me + i, BLOCKS) for i in indices]
+        for b in blocks:
+            rows = result[order[b]].astype(jnp.bfloat16)
+            o_buf[b] = jnp.concatenate([rows[j * ROWS : (j + 1) * ROWS] for j in range(GROUP)], axis=1)
+        for i, b in zip(indices, blocks):
+
+            @pl.when(i < BLOCKS)
+            def _():
+                pltpu.make_async_remote_copy(
+                    src_ref=o_buf.at[b], dst_ref=out_copy(b, part),
+                    send_sem=o_send, recv_sem=o_recv,
+                    device_id=plane_device(b), device_id_type=MESH,
+                ).start()
 
         return carry
 
-    lax.fori_loop(1, BLOCKS + 1, send_back, 0)
+    lax.fori_loop(0, BLOCKS // 4, send_back, 0)
     own_o = pltpu.make_async_copy(o_buf.at[me], out_copy(me, part), o_own)
     own_o.start()
 
@@ -362,11 +427,13 @@
     pltpu.make_async_copy(many_q, many_q, q_send).wait()
     pltpu.make_async_copy(many, many, kv_send).wait()
     for distance in range(1, 5):
-        for turn in range(0, PIECES, 1 if distance < 4 else 2):
+        for turn in range(0, TURNS, 1 if distance < 4 else 2):
             ring(distance, True, turn).wait_send()
             ring(distance, False, turn).wait_send()
-    for step in range(10):
-        across(step, z, 0, 4 if 2 <= step < 8 else 2).wait_send()
+        if distance < 4:
+            over(distance, z, 0, 2).wait_send()
+    for step in range(11):
+        across(step, z, 0, 4 if step in (2, 3, 4, 5, 7) else 2).wait_send()
     own_o.wait()
     pltpu.make_async_copy(many_o, many_o, o_send).wait()
     pltpu.make_async_copy(many_o, many_o, o_recv).wait()
@@ -396,7 +463,7 @@
             pltpu.VMEM((BLOCKS, ROWS, WIDE), jnp.bfloat16),
             pltpu.SMEM((BLOCKS,), jnp.int32),
             dma((3,)), dma, dma, dma, dma, dma, dma,
-            *[dma((4 * PIECES,))] * 4, dma((10,)), dma((10,)),
+            *[dma((4 * TURNS,))] * 4, dma((11,)), dma((11,)), dma((3,)), dma((3,)),
             dma, dma, dma,
         ],
         compiler_params=pltpu.CompilerParams(

time: 55.1 us -> 53.6 us (0.973)
  Pallas kernels: 54.1 us -> 52.7 us
    pallas_call x1, Pallas kernels: 54.1 us -> 52.7 us  [shards(): pl.pallas_call(kernel, out_shape=pltpu.VMEM((PART // ROWS, ROWS, 8 * WIDE...]
where the time goes in v3:
time: 53.6 us; the launch traced here: 53.5 us
  Pallas kernels  52.7 us (98%)
  local copies, waits for them, and re-layouts  0.77 us (1%)
    pallas_call x1, Pallas kernels, shards(): pl.pallas_call(kernel, out_shape=pltpu.VMEM((PART // ROWS, ROWS, 8 * WIDE...  52.7 us

profile of v3, /device:TPU:25, one launch (start us, length us, event | category | flops | bytes accessed | tf_op | source)
XLA Modules:
  0.0 53.5 jit_solution(5310802765373335642)
XLA Ops:
  0.0 52.7 %shard_map.46 = bf16[4,8,7168]{2,1,0:T(8,128)(2,1)S(1)} custom-call(s32[32]{0:T(128)} %order.1, bf16[4,8,7168]{2,1,0:T(8,128)(2,1)} %bitcast.3, bf16[32,1024]{1,0:T(8,128)(2,1)} %k_in.1, bf16[32,1024]{1,0:T(8,128)(2,1)} %v_in.1), custom_call_target="tpu_custom_call" | custom-call | flops 3758096384 | bytes 2097152 | tf_op jit(solution)/shard_map/pallas_call | solution.py:445
  52.7 0.8 %copy.6 = bf16[32,7168]{1,0:T(8,128)(2,1)} copy(bf16[32,7168]{1,0:T(8,128)(2,1)S(1)} %bitcast.2) | data formatting | bytes 917504

commit v4 on v3

--- a/solution.py
+++ b/solution.py
@@ -164,27 +164,18 @@
         )
 
     def pass_on(distance, turn):
-        ring(distance, True, turn).wait_recv()
-        ring(distance, False, turn).wait_recv()
-
-        @pl.when((distance < 3) | (distance == 3) & (turn != 1))
-        def _():
-            ring(distance + 1, True, turn).start()
-            ring(distance + 1, False, turn).start()
-
-        lower, upper = lax.rem(z + PLANES - distance, PLANES), lax.rem(z + distance, PLANES)
-        if turn == 2:
-
-            @pl.when(distance < 4)
-            def _():
-                for chunk, upward in ((lower, True), (upper, False)):
-                    over(distance, chunk, piece_of(upward, 2)).start()
-
         step = 2 * distance + turn // 2
         if turn == 0:
             step = jnp.where(distance == 3, 10, step)
-        across(step, lower, piece_of(True, turn)).start()
-        across(step, upper, piece_of(False, turn)).start()
+        for upward in (True, False):
+            chunk = lax.rem(z + (PLANES - distance if upward else distance), PLANES)
+            ring(distance, upward, turn).wait_recv()
+            if turn == 2:
+                pl.when(distance < 4)(lambda: over(distance, chunk, piece_of(upward, 2)).start())
+            pl.when((distance < 3) | (distance == 3) & (turn != 1))(
+                lambda: ring(distance + 1, upward, turn).start()
+            )
+            across(step, chunk, piece_of(upward, turn)).start()
 
     def over(distance, chunk, first, count=1):
         held = kv.at[chunk, core, pl.ds(first * PIECE, count * PIECE)]

time: 53.6 us -> 53.4 us (level)
  no operation moved by 1% of the time
where the time goes in v4:
time: 53.4 us; the launch traced here: 53.3 us
  Pallas kernels  52.5 us (98%)
  local copies, waits for them, and re-layouts  0.77 us (1%)
    pallas_call x1, Pallas kernels, shards(): pl.pallas_call(kernel, out_shape=pltpu.VMEM((PART // ROWS, ROWS, 8 * WIDE...  52.5 us

profile of v4, /device:TPU:25, one launch (start us, length us, event | category | flops | bytes accessed | tf_op | source)
XLA Modules:
  0.0 53.3 jit_solution(15331771545099071788)
XLA Ops:
  0.0 52.5 %shard_map.46 = bf16[4,8,7168]{2,1,0:T(8,128)(2,1)S(1)} custom-call(s32[32]{0:T(128)} %order.1, bf16[4,8,7168]{2,1,0:T(8,128)(2,1)} %bitcast.3, bf16[32,1024]{1,0:T(8,128)(2,1)} %k_in.1, bf16[32,1024]{1,0:T(8,128)(2,1)} %v_in.1), custom_call_target="tpu_custom_call" | custom-call | flops 3758096384 | bytes 2097152 | tf_op jit(solution)/shard_map/pallas_call | solution.py:436
  52.5 0.8 %copy.6 = bf16[32,7168]{1,0:T(8,128)(2,1)} copy(bf16[32,7168]{1,0:T(8,128)(2,1)S(1)} %bitcast.2) | data formatting | bytes 917504

commit v5 on v4

--- a/solution.py
+++ b/solution.py
@@ -310,6 +310,16 @@
                 between[i]()
         add(*before)
 
+    def finish(t):
+        total = acc[t]
+        rows = (total[:HD] * (1.0 / total[HD : HD + 1])).T
+        at = t * TILE
+        while at < (t + 1) * TILE:
+            block, row = at // QROWS, at % QROWS
+            count = min(QROWS - row, (t + 1) * TILE - at)
+            result[block, row : row + count, :] = rows[at - t * TILE : at - t * TILE + count]
+            at += count
+
     def one_distance(distance, carry):
         lower, upper = lax.rem(z + PLANES - distance, PLANES), lax.rem(z + distance, PLANES)
         alone = (distance == 0) | (distance == 4)
@@ -372,7 +382,8 @@
         @pl.when(distance > 1)
         def _():
             from_sibling(2 * distance - 1, 4)
-            attend(high(lax.rem(lower + 1, PLANES), lax.rem(upper + PLANES - 1, PLANES)))
+            early = {t: lambda t=t: finish(t) for t in range(TILES) if SPAN[t][1] <= HALF}
+            attend(high(lax.rem(lower + 1, PLANES), lax.rem(upper + PLANES - 1, PLANES)), early)
             pl.when(distance == 3)(lambda: from_sibling(8, 2))
 
         return carry
@@ -380,14 +391,8 @@
     lax.fori_loop(0, 5, one_distance, 0)
 
     for t in range(TILES):
-        total = acc[t]
-        rows = (total[:HD] * (1.0 / total[HD : HD + 1])).T
-        at = t * TILE
-        while at < (t + 1) * TILE:
-            block, row = at // QROWS, at % QROWS
-            count = min(QROWS - row, (t + 1) * TILE - at)
-            result[block, row : row + count, :] = rows[at - t * TILE : at - t * TILE + count]
-            at += count
+        if SPAN[t][1] > HALF:
+            finish(t)
 
     def out_copy(b, device_rows):
         return out.at[device_rows, :, pl.ds(pl.multiple_of(g * WIDE, HD), WIDE)]

time: 53.4 us -> 53.4 us (level)
  no operation moved by 1% of the time
where the time goes in v5:
time: 53.4 us; the launch traced here: 53.3 us
  Pallas kernels  52.6 us (99%)
  local copies, waits for them, and re-layouts  0.77 us (1%)
    pallas_call x1, Pallas kernels, shards(): pl.pallas_call(kernel, out_shape=pltpu.VMEM((PART // ROWS, ROWS, 8 * WIDE...  52.6 us

profile of v5, /device:TPU:25, one launch (start us, length us, event | category | flops | bytes accessed | tf_op | source)
XLA Modules:
  0.0 53.3 jit_solution(1421400435288514430)
XLA Ops:
  0.0 52.6 %shard_map.46 = bf16[4,8,7168]{2,1,0:T(8,128)(2,1)S(1)} custom-call(s32[32]{0:T(128)} %order.1, bf16[4,8,7168]{2,1,0:T(8,128)(2,1)} %bitcast.3, bf16[32,1024]{1,0:T(8,128)(2,1)} %k_in.1, bf16[32,1024]{1,0:T(8,128)(2,1)} %v_in.1), custom_call_target="tpu_custom_call" | custom-call | flops 3758096384 | bytes 2097152 | tf_op jit(solution)/shard_map/pallas_call | solution.py:441
  52.6 0.8 %copy.6 = bf16[32,7168]{1,0:T(8,128)(2,1)} copy(bf16[32,7168]{1,0:T(8,128)(2,1)S(1)} %bitcast.2) | data formatting | bytes 917504
